TPU v7x, 32 devices: a whole 2x2x4 slice. The times are simulated.
32 devices in a mesh: wide: 16 (over z, y, x), deep: 2 (over core).
Axes of the slice: x: 2, y: 2, z: 4, core: 2. Of those that a mesh axis runs over, the one named last changes fastest.
Arguments:
- right_side: float32 [32, 128, 256], P('wide', 'deep'), may hold values from -12 to 12
- conductivity: float32 [32, 128, 256], P('wide', 'deep'), may hold values from 0.2 to 5
- checksum_weights: int32 [2, 16], replicated, may hold values from 1 to 15
- holder: int32 [16], replicated, may hold values from 0 to 15, as said below
Outputs:
- solution_field: float32 [32, 128, 256], P('wide', 'deep')
- residual: float32 [32, 128, 256], P('wide', 'deep')
- stored: float32 [32, 4, 4096], P('wide', None, 'deep')
Inputs may be any that keep to these rules, and one draw needn't show every extreme that they name: No holder takes more than 2 pieces, and some take exactly 2; others take fewer or none.
All inputs are finite; a program needn't handle non-finite values.
Results may differ from a plain program's by a relative error of at most 0.00017.
Values sent between devices are 32-bit elements; how exact they have to be, the bound alone decides.
A program may use at most 64 MiB of HBM per device.

v0:
```python
import jax
import jax.numpy as jnp
from jax import lax
from jax.sharding import PartitionSpec as P

ITERS = 3
HOLD = 2


OFFSETS = tuple(
    (
        (a, b, c)
        for a in (-1, 0, 1)
        for b in (-1, 0, 1)
        for c in (-1, 0, 1)
        if (a, b, c) != (0, 0, 0)
    )
)


def with_halo(array, sides, width):
    for axis, dim in sides:
        size, length = (lax.axis_size(axis), array.shape[dim])
        up = [(i, (i + 1) % size) for i in range(size - 1)]
        down = [(j, i) for i, j in up]
        last = lax.slice_in_dim(array, length - width, length, axis=dim)
        leading = lax.slice_in_dim(array, 0, width, axis=dim)
        before = lax.ppermute(last, axis, up)
        after = lax.ppermute(leading, axis, down)
        array = jnp.concatenate([before, array, after], axis=dim)
    return array


def coupling(offset):
    return (1.0, 0.5, 0.25)[abs(offset[0]) + abs(offset[1]) + abs(offset[2]) - 1]


def neighbour(padded, offset, planes_x, planes_y):
    plane = padded[
        1 + offset[0] : 1 + offset[0] + planes_x, 1 + offset[1] : 1 + offset[1] + planes_y, :
    ]
    if offset[2] == 0:
        return plane
    zeros = jnp.zeros_like(plane[:, :, :1])
    if offset[2] == 1:
        return jnp.concatenate([plane[:, :, 1:], zeros], axis=2)
    return jnp.concatenate([zeros, plane[:, :, :-1]], axis=2)


def operate(field, conductivity, padded_conductivity, diagonal):
    planes_x, planes_y = (field.shape[0], field.shape[1])
    padded = with_halo(field, (("wide", 0), ("deep", 1)), 1)
    total = diagonal * field
    for offset in OFFSETS:
        weight = (
            coupling(offset)
            * 0.5
            * (conductivity + neighbour(padded_conductivity, offset, planes_x, planes_y))
        )
        total = total - weight * neighbour(padded, offset, planes_x, planes_y)
    return total


def classic_norm(residual, precond):
    return lax.psum(jnp.sum(residual * precond), ("wide", "deep"))


def body(right_side, conductivity, checksum_weights, holder):
    planes_x, planes_y = (conductivity.shape[0], conductivity.shape[1])
    padded_conductivity = with_halo(conductivity, (("wide", 0), ("deep", 1)), 1)
    diagonal = jnp.zeros_like(conductivity)
    for offset in OFFSETS:
        diagonal = diagonal + coupling(offset) * 0.5 * (
            conductivity + neighbour(padded_conductivity, offset, planes_x, planes_y)
        )
    solution_field = jnp.zeros_like(right_side)
    residual = right_side
    precond = residual / diagonal
    direction = precond
    product_now = classic_norm(residual, precond)
    for iteration in range(ITERS):
        image = operate(direction, conductivity, padded_conductivity, diagonal)
        step_length = product_now / lax.psum(jnp.sum(direction * image), ("wide", "deep"))
        solution_field = solution_field + step_length * direction
        residual = residual - step_length * image
        precond = residual / diagonal
        product_next = classic_norm(residual, precond)
        direction = precond + product_next / product_now * direction
        product_now = product_next
    width = lax.axis_size("wide")
    position = lax.axis_index("wide")
    weights_float = checksum_weights.astype(jnp.float32)
    scales = 1.0 / jnp.sqrt(jnp.sum(weights_float * weights_float, axis=1))
    scaled_weights = weights_float * scales[:, None]
    checks_count = checksum_weights.shape[0]
    flat = jnp.stack([solution_field, direction]).reshape(2, -1)
    cells = flat.shape[1]
    mine = lax.dynamic_slice_in_dim(scaled_weights, position, 1, 1)[:, 0]
    terms = (flat[:, None, :] * mine[None, :, None]).reshape(2 * checks_count, cells)
    piece = lax.psum_scatter(terms, "wide", scatter_dimension=1, tiled=True)
    index_range = jnp.arange(width, dtype=jnp.int32)
    same = holder[:, None] == holder[None, :]
    earlier = index_range[:, None] < index_range[None, :]
    slots = jnp.sum((same & earlier).astype(jnp.int32), axis=0)
    slot_range = jnp.arange(HOLD, dtype=jnp.int32)
    select = ((holder[None, :] == position) & (slots[None, :] == slot_range[:, None])).astype(
        jnp.float32
    )
    target = (index_range == holder[position]).astype(jnp.float32)
    outgoing = target[:, None, None] * piece[None, :, :]
    arrived = lax.all_to_all(outgoing, "wide", split_axis=0, concat_axis=0, tiled=True)
    stored = jnp.einsum("sj,jfc->sfc", select, arrived, precision=lax.Precision.HIGHEST)
    return (solution_field, residual, stored)


def solution(mesh):
    placed = (P("wide", "deep", None), P("wide", "deep", None), P(), P())
    return jax.shard_map(
        body,
        mesh=mesh,
        in_specs=placed,
        out_specs=(P("wide", "deep", None), P("wide", "deep", None), P("wide", None, "deep")),
        check_vma=False,
    )
```

profile of v0, /device:TPU:0, one launch (start us, length us, event | category | flops | bytes accessed | tf_op | source)
XLA Modules:
  0.0 740.2 jit_solution(2632055515943454148)
XLA Ops:
  8.1 4.8 collective-permute-start
  16.3 2.8 collective-permute-done.1
  23.8 1.7 fusion.145
  26.9 4.9 collective-permute-start.4
  32.3 2.7 collective-permute-done.4
  39.7 1.9 multiply_reduce_fusion.5
  41.6 44.4 %all-reduce.72 = (f32[]{:T(128)}, f32[]{:T(128)}) all-reduce(f32[]{:T(128)} %get-tuple-element.13, f32[]{:T(128)} %get-tuple-element.12), channel_id=1, replica_groups=mesh['wide'=16,'deep'=2] {'wide','deep'}, use_global_device_ids=true, to_apply=%region_1.0 | all-reduce | flops 2 | bytes 16 | tf_op jit(solution)/shard_map/psum | solution.py:65
  87.4 2.2 multiply_reduce_fusion.4
  89.6 40.1 %psum.51 = f32[]{:T(128)} all-reduce(f32[]{:T(128)} %get-tuple-element.26), channel_id=1, replica_groups=mesh['wide'=16,'deep'=2] {'wide','deep'}, use_global_device_ids=true, to_apply=%region_5.0 | all-reduce | flops 1 | bytes 8 | tf_op jit(solution)/shard_map/psum | solution.py:65
  133.4 4.8 collective-permute-start.8
  138.5 2.2 collective-permute-done.8
  145.4 2.9 multiply_reduce_fusion.3
  148.4 44.4 %psum.52 = f32[]{:T(128)} all-reduce(f32[]{:T(128)} %get-tuple-element.24), channel_id=1, replica_groups=mesh['wide'=16,'deep'=2] {'wide','deep'}, use_global_device_ids=true, to_apply=%region_7.0 | all-reduce | flops 1 | bytes 8 | tf_op jit(solution)/shard_map/psum | solution.py:83
  194.0 2.4 multiply_reduce_fusion.2
  196.3 39.0 %psum.53 = f32[]{:T(128)} all-reduce(f32[]{:T(128)} %get-tuple-element.21), channel_id=1, replica_groups=mesh['wide'=16,'deep'=2] {'wide','deep'}, use_global_device_ids=true, to_apply=%region_9.0 | all-reduce | flops 1 | bytes 8 | tf_op jit(solution)/shard_map/psum | solution.py:65
  239.6 5.4 collective-permute-start.12
  253.0 3.0 multiply_reduce_fusion.1
  256.0 45.2 %psum.54 = f32[]{:T(128)} all-reduce(f32[]{:T(128)} %get-tuple-element.19), channel_id=1, replica_groups=mesh['wide'=16,'deep'=2] {'wide','deep'}, use_global_device_ids=true, to_apply=%region_11.0 | all-reduce | flops 1 | bytes 8 | tf_op jit(solution)/shard_map/psum | solution.py:83
  302.6 2.2 multiply_reduce_fusion
  304.9 39.5 %psum.55 = f32[]{:T(128)} all-reduce(f32[]{:T(128)} %get-tuple-element.16), channel_id=1, replica_groups=mesh['wide'=16,'deep'=2] {'wide','deep'}, use_global_device_ids=true, to_apply=%region_14.0 | all-reduce | flops 1 | bytes 8 | tf_op jit(solution)/shard_map/psum | solution.py:65
  347.4 8.6 %copy.12 = f32[4,32768]{0,1:T(8,128)} copy(f32[4,32768]{1,0:T(4,128)S(1)} %broadcast_multiply_fusion.1) | data formatting | bytes 1048576
  357.2 346.3 %reduce-scatter.4.cloned.1.call-done = f32[2048,4]{1,0:T(8,128)} async-done(((f32[32768,4]{1,0:T(8,128)}), f32[2048,4]{1,0:T(8,128)}) %reduce-scatter.4.cloned.1.call-update) | async-done | bytes 32784
  706.1 11.2 %all-to-all-start = ((f32[16,4,2048]{2,1,0:T(4,128)}), f32[16,4,2048]{2,1,0:T(4,128)S(1)}, u32[]{:S(2)}, u32[]{:S(2)}) async-start(f32[16,4,2048]{2,1,0:T(4,128)} %broadcast_multiply_fusion), calls=%async_computation | async-start | bytes 1048576 | tf_op jit(solution)/shard_map/all_to_all | solution.py:111
  717.4 14.7 %all-to-all-done = f32[16,4,2048]{2,1,0:T(4,128)S(1)} async-done(((f32[16,4,2048]{2,1,0:T(4,128)}), f32[16,4,2048]{2,1,0:T(4,128)S(1)}, u32[]{:S(2)}, u32[]{:S(2)}) %all-to-all-start) | async-done | bytes 524320 | tf_op jit(solution)/shard_map/all_to_all | solution.py:111
  (92 shorter events, 40.0 us)
Async XLA Ops:
  7.2 32.5 %copy-start.3 = (f32[2,64,256]{2,1,0:T(8,128)S(1)}, f32[2,64,256]{2,1,0:T(8,128)}, u32[]{:S(2)}) copy-start(f32[2,64,256]{2,1,0:T(8,128)} %param.4) | copy-start | bytes 393220
  7.2 131.0 %copy-start.5 = (s32[2,16]{1,0:T(2,128)S(1)}, s32[2,16]{1,0:T(2,128)}, u32[]{:S(2)}) copy-start(s32[2,16]{1,0:T(2,128)} %param.6) | copy-start | bytes 388
  7.2 696.4 %reduce-scatter.4.cloned.1.call-start = ((), (), s32[]{:S(2)}) async-start(), calls=%async_computation.2 | async-start | bytes 17825792
  8.1 7.2 collective-permute-start
  13.0 6.2 collective-permute-start.1
  19.2 2.8 collective-permute-start.2
  20.6 3.1 collective-permute-start.3
  25.5 16.1 %copy-start.1 = (f32[2,64,256]{2,1,0:T(8,128)}, f32[2,64,256]{2,1,0:T(8,128)S(1)}, u32[]{:S(2)}) copy-start(f32[2,64,256]{2,1,0:T(8,128)S(1)} %get-tuple-element.56) | copy-start | bytes 393220
  25.5 16.1 %copy-start.2 = (f32[2,64,256]{2,1,0:T(8,128)}, f32[2,64,256]{2,1,0:T(8,128)S(1)}, u32[]{:S(2)}) copy-start(f32[2,64,256]{2,1,0:T(8,128)S(1)} %get-tuple-element.57) | copy-start | bytes 393220
  25.5 211.1 %copy-start = (f32[2,64,256]{2,1,0:T(8,128)}, f32[2,64,256]{2,1,0:T(8,128)S(1)}, u32[]{:S(2)}) copy-start(f32[2,64,256]{2,1,0:T(8,128)S(1)} %get-tuple-element.55) | copy-start | bytes 393220
  25.6 6.7 collective-permute-start.5
  26.9 8.1 %collective-permute-start.4 = (f32[1,64,256]{2,1,0:T(8,128)S(1)}, f32[1,64,256]{2,1,0:T(8,128)S(1)}, u32[]{:S(2)}, u32[]{:S(2)}) collective-permute-start(f32[1,64,256]{2,1,0:T(8,128)S(1)} %get-tuple-element.140), channel_id=1, source_target_pairs={{0,2},{2,4},{4,6},{6,8},{8,10},{10,12},{12,14},{14,16},{16,18},{18... | collective-permute-start | bytes 196616 | tf_op jit(solution)/shard_map/ppermute | solution.py:28
  35.0 2.7 collective-permute-start.6
  36.3 3.1 collective-permute-start.7
  132.1 6.4 collective-permute-start.9
  133.4 7.3 collective-permute-start.8
  140.7 2.7 collective-permute-start.10
  142.0 3.1 collective-permute-start.11
  238.3 7.1 collective-permute-start.13
  239.6 7.0 collective-permute-start.12
  247.3 3.6 collective-permute-start.14
  248.6 3.1 collective-permute-start.15
  345.8 10.1 %copy-start.4 = (f32[2,64,256]{2,1,0:T(8,128)}, f32[2,64,256]{2,1,0:T(8,128)S(1)}, u32[]{:S(2)}) copy-start(f32[2,64,256]{2,1,0:T(8,128)S(1)} %get-tuple-element.123) | copy-start | bytes 393220
  706.1 26.1 %all-to-all-start = ((f32[16,4,2048]{2,1,0:T(4,128)}), f32[16,4,2048]{2,1,0:T(4,128)S(1)}, u32[]{:S(2)}, u32[]{:S(2)}) async-start(f32[16,4,2048]{2,1,0:T(4,128)} %broadcast_multiply_fusion), calls=%async_computation | async-start | bytes 1048576 | tf_op jit(solution)/shard_map/all_to_all | solution.py:111
  (1 other events, 8.6 us)
Sparse Core Ops, SparseCore 0:
  356.1 347.4 reduce-scatter.3
where the time goes:
time: 742 us; the launch traced here: 740 us
  waiting for transfers between devices  376 us (51%)
  blocking collectives  253 us (34%)
  starting transfers between devices  46.8 us (6%)
  other arithmetic  23.8 us (3%)
  between operations  22.6 us (3%)
  local copies, waits for them, and re-layouts  17.6 us (2%)
    unnamed x2, waiting for transfers between devices  346 us
    psum x4, blocking collectives, classic_norm(): return lax.psum(jnp.sum(residual * precond), ('wide', 'deep'))  163 us
    psum x2, blocking collectives, body(): lax.psum(jnp.sum(direction * image), ('wide', 'deep'))  89.6 us
    ppermute x8, starting transfers between devices, with_halo(): before = lax.ppermute(last, axis, up)  25.2 us
  transfers between devices with their start and end apart: 18, of which 12 were waited for; matrix products, arithmetic and copies ran while one was open for 1% of the time, Pallas kernels for 0%

commit v1 on v0

v1 whole, which is shorter than its diff:
```python
import functools

import jax
import jax.numpy as jnp
from jax import lax
from jax.experimental import pallas as pl
from jax.experimental.pallas import tpu as pltpu
from jax.sharding import PartitionSpec as P

ITERS = 3
HOLD = 2
PAD = 8
LANES = 128
SIDES = ((1, 0), (-1, 0), (0, 1), (0, -1), (1, 1), (1, -1), (-1, 1), (-1, -1))
MESH = pl.DeviceIdType.MESH


def span(step, source, count):
    if step == 0:
        return pl.ds(1, count)
    if source:
        return pl.ds(count if step > 0 else 1, 1)
    return pl.ds(0 if step > 0 else count + 1, 1)


def rows_of(step, source, count):
    if step == 0:
        return pl.ds(PAD, count)
    if source:
        return pl.ds(count if step > 0 else PAD, PAD)
    return pl.ds(0 if step > 0 else PAD + count, PAD)


def kernel(wide, deep, pieces, *refs):
    r_ref, k_ref, w_ref, h_ref = refs[:4]
    x_out, res_out, last_out = refs[4:7]
    (ext, zed, dirn, halo_send, halo_recv, pair, line, sum_send, sum_recv) = refs[7:16]
    planes, rows, cols = k_ref.shape
    w = lax.axis_index("wide")
    d = lax.axis_index("deep")

    def there(dx, dy):
        return (w + dx >= 0) & (w + dx < wide) & (d + dy >= 0) & (d + dy < deep)

    barrier = pltpu.get_barrier_semaphore()

    def greet_wide(i, carry):
        pl.semaphore_signal(barrier, inc=1, device_id=(lax.rem(w + i, wide), d), device_id_type=MESH)
        return carry

    def greet_deep(i, carry):
        pl.semaphore_signal(barrier, inc=1, device_id=(w, lax.rem(d + i, deep)), device_id_type=MESH)
        return carry

    lax.fori_loop(1, wide, greet_wide, 0)
    lax.fori_loop(1, deep, greet_deep, 0)
    greeted = jnp.int32(wide + deep - 2)
    for dx, dy in SIDES[4:]:
        there_now = there(dx, dy)
        greeted = greeted + jnp.where(there_now, 1, 0)

        @pl.when(there_now)
        def _():
            pl.semaphore_signal(barrier, inc=1, device_id=(w + dx, d + dy), device_id_type=MESH)

    for phase in range(4):
        for dx, dy in SIDES:

            @pl.when(jnp.logical_not(there(-dx, -dy)))
            def _():
                at = (phase, span(dx, False, planes), rows_of(dy, False, rows))
                ext[at] = jnp.zeros_like(ext[at])

    inner = (slice(1, planes + 1), slice(PAD, PAD + rows))
    ext[(0,) + inner] = k_ref[...]

    if pieces:
        (field, parts, landed, sums, chosen, choose, final, all_send, all_recv) = refs[16:]
        lane = lax.broadcasted_iota(jnp.int32, (1, 4 * wide), 1)
        place = jnp.zeros((1, 4 * wide), jnp.int32)
        hold = [h_ref[j] for j in range(wide)]
        for j in range(wide):
            slot = jnp.int32(0)
            for i in range(j):
                slot = slot + jnp.where(hold[i] == hold[j], 1, 0)
            place = jnp.where(lane % wide == j, hold[j] * HOLD + slot, place)
        line_no = lax.broadcasted_iota(jnp.int32, (8 * wide, 4 * wide), 0)
        lane_no = lax.broadcasted_iota(jnp.int32, (8 * wide, 4 * wide), 1)
        hit = (line_no // 4 == place) & (line_no % 4 == lane_no // wide)
        choose[...] = jnp.where(hit, 1.0, 0.0).astype(jnp.float32)

    def halo_copy(phase, side):
        dx, dy = SIDES[side]
        return pltpu.make_async_remote_copy(
            src_ref=ext.at[phase, span(dx, True, planes), rows_of(dy, True, rows)],
            dst_ref=ext.at[phase, span(dx, False, planes), rows_of(dy, False, rows)],
            send_sem=halo_send.at[phase, side],
            recv_sem=halo_recv.at[phase, side],
            device_id=(w + dx, d + dy),
            device_id_type=MESH,
        )

    def halo_start(phase):
        for side, (dx, dy) in enumerate(SIDES):

            @pl.when(there(dx, dy))
            def _():
                halo_copy(phase, side).start()

    def halo_wait(phase):
        for side, (dx, dy) in enumerate(SIDES):

            @pl.when(there(-dx, -dy))
            def _():
                halo_copy(phase, side).wait_recv()

    def halo_sent(phase):
        for side, (dx, dy) in enumerate(SIDES):

            @pl.when(there(dx, dy))
            def _():
                halo_copy(phase, side).wait_send()

    col = lax.broadcasted_iota(jnp.int32, (rows, cols), 1)

    def smooth(block):
        result = []
        for x in range(planes):
            t = 0.5 * (block[x] + block[x + 2]) + block[x + 1]
            tall = t.shape[0]
            t = 0.5 * (pltpu.roll(t, 1, 0) + pltpu.roll(t, tall - 1, 0)) + t
            t = t[PAD:PAD + rows]
            left = jnp.where(col == 0, 0.0, pltpu.roll(t, 1, 1))
            right = jnp.where(col == cols - 1, 0.0, pltpu.roll(t, cols - 1, 1))
            result.append(0.5 * (left + right) + t)
        return result

    pl.semaphore_wait(barrier, greeted)
    halo_start(0)
    halo_wait(0)

    kappa = [ext[0, x] for x in range(planes + 2)]
    blurred = smooth(kappa)
    mine = [k_ref[x] for x in range(planes)]
    diagonal = [6.0 * mine[x] + blurred[x] for x in range(planes)]
    inverse = [1.0 / diagonal[x] for x in range(planes)]
    for x in range(planes):
        ext[1, x + 1, PAD:PAD + rows] = r_ref[x] * inverse[x]
    halo_start(1)
    halo_wait(1)

    lane1 = lax.broadcasted_iota(jnp.int32, (1, LANES), 1)

    def total_of(turn, values):
        row = jnp.zeros((1, LANES), jnp.float32)
        for i, value in enumerate(values):
            one = value[0]
            for x in range(1, planes):
                one = one + value[x]
            one = jnp.sum(jnp.sum(one, axis=0, keepdims=True), axis=1, keepdims=True)
            row = jnp.where(lane1 == i, one, row)
        pair[turn, d] = row

        def to_deep(i, carry):
            pltpu.make_async_remote_copy(
                src_ref=pair.at[turn, d], dst_ref=pair.at[turn, d],
                send_sem=sum_send.at[turn, 0], recv_sem=sum_recv.at[turn, 0],
                device_id=(w, lax.rem(d + i, deep)), device_id_type=MESH,
            ).start()
            return carry

        lax.fori_loop(1, deep, to_deep, 0)
        some = pair.at[turn, pl.ds(0, deep - 1)]
        pltpu.make_async_copy(some, some, sum_recv.at[turn, 0]).wait()
        row = pair[turn, 0]
        for i in range(1, deep):
            row = row + pair[turn, i]
        line[turn, w] = row

        def to_wide(i, carry):
            pltpu.make_async_remote_copy(
                src_ref=line.at[turn, w], dst_ref=line.at[turn, w],
                send_sem=sum_send.at[turn, 1], recv_sem=sum_recv.at[turn, 1],
                device_id=(lax.rem(w + i, wide), d), device_id_type=MESH,
            ).start()
            return carry

        lax.fori_loop(1, wide, to_wide, 0)
        some = line.at[turn, pl.ds(0, wide - 1)]
        pltpu.make_async_copy(some, some, sum_recv.at[turn, 1]).wait()
        row = jnp.sum(line[turn], axis=0)
        return [row[:, i:i + 1] for i in range(len(values))]

    for turn in range(ITERS):
        before = 1 if turn == 0 else None
        block = [ext[1, x] if before else dirn[x] for x in range(planes + 2)]
        own = [block[x + 1][PAD:PAD + rows] for x in range(planes)]
        first = smooth(block)
        second = smooth([ext[0, x] * block[x] for x in range(planes + 2)])
        image, spread = [], []
        for x in range(planes):
            k = k_ref[x]
            image.append((diagonal[x] + 2.0 * k) * own[x] - k * first[x] - second[x])
            spread.append(image[x] * inverse[x])
        carries_on = turn < ITERS - 1
        if carries_on:
            for x in range(planes):
                ext[turn + 2, x + 1, PAD:PAD + rows] = spread[x]
            halo_start(turn + 2)
        rest = [r_ref[x] if turn == 0 else res_out[x] for x in range(planes)]
        if turn == 0:
            near = own
        else:
            near = [zed[x + 1, PAD:PAD + rows] for x in range(planes)]
        both = range(planes)
        rz, pq, zq, qq = total_of(turn, [
            [rest[x] * near[x] for x in both],
            [own[x] * image[x] for x in both],
            [rest[x] * spread[x] for x in both],
            [image[x] * spread[x] for x in both],
        ])
        step = rz / pq
        later = rz - 2.0 * step * zq + step * step * qq
        ratio = later / rz
        for x in both:
            base = step * own[x]
            x_out[x] = base if turn == 0 else x_out[x] + base
            res_out[x] = rest[x] - step * image[x]
        if carries_on:
            halo_wait(turn + 2)
            for x in range(planes + 2):
                old = ext[1, x] if turn == 0 else zed[x]
                new = old - step * ext[turn + 2, x]
                zed[x] = new
                dirn[x] = new + ratio * block[x]
        else:
            final_dirn = [near[x] - step * spread[x] + ratio * own[x] for x in both]

    if pieces:
        halves = cols // LANES
        for f in range(2):
            for x in range(planes):
                value = x_out[x] if f == 0 else final_dirn[x]
                for s in range(halves):
                    field[f, s, x * rows:(x + 1) * rows] = value[:, s * LANES:(s + 1) * LANES]
        stride = planes * rows // wide
        for c in range(wide):
            for f in range(2):
                parts[c, f * wide:(f + 1) * wide] = field[
                    f, c % halves, pl.ds(c // halves, wide, stride=stride), :]
        landed[w] = parts[w]

        def scatter(i, carry):
            q = lax.rem(w + i, wide)
            pltpu.make_async_remote_copy(
                src_ref=parts.at[q], dst_ref=landed.at[w],
                send_sem=all_send.at[0], recv_sem=all_recv.at[0],
                device_id=(q, d), device_id_type=MESH,
            ).start()
            return carry

        lax.fori_loop(1, wide, scatter, 0)
        some = landed.at[pl.ds(0, wide - 1)]
        pltpu.make_async_copy(some, some, all_recv.at[0]).wait()
        for k in range(2):
            squares = jnp.int32(0)
            for p in range(wide):
                squares = squares + w_ref[k, p] * w_ref[k, p]
            scale = 1.0 / jnp.sqrt(jnp.full((1, LANES), squares.astype(jnp.float32)))
            for f in range(2):
                total = jnp.zeros((wide, LANES), jnp.float32)
                for p in range(wide):
                    total = total + w_ref[k, p].astype(jnp.float32) * landed[p, f * wide:(f + 1) * wide]
                at = (2 * f + k) * wide
                sums[at:at + wide] = total * scale
        chosen[...] = jnp.dot(
            choose[...], sums[...], precision=lax.Precision.HIGHEST,
            preferred_element_type=jnp.float32)

        def slot_rows(q):
            return pl.ds(pl.multiple_of(q * 8, 8), 8)

        here = pl.ds(pl.multiple_of(w * LANES, LANES), LANES)
        final[:, here] = chosen[slot_rows(w), :]

        def deliver(i, carry):
            q = lax.rem(w + i, wide)
            pltpu.make_async_remote_copy(
                src_ref=chosen.at[slot_rows(q)], dst_ref=final.at[:, here],
                send_sem=all_send.at[1], recv_sem=all_recv.at[1],
                device_id=(q, d), device_id_type=MESH,
            ).start()
            return carry

        lax.fori_loop(1, wide, deliver, 0)
        some = final.at[:, pl.ds(0, (wide - 1) * LANES)]
        pltpu.make_async_copy(some, some, all_recv.at[1]).wait()
        last_out[...] = final[...]
        some = parts.at[pl.ds(0, wide - 1)]
        pltpu.make_async_copy(some, some, all_send.at[0]).wait()
        some = chosen.at[pl.ds(0, (wide - 1) * 8)]
        pltpu.make_async_copy(some, some, all_send.at[1]).wait()
    else:
        for x in range(planes):
            last_out[x] = final_dirn[x]

    for phase in range(4):
        halo_sent(phase)
    for turn in range(ITERS):
        some = pair.at[turn, pl.ds(0, deep - 1)]
        pltpu.make_async_copy(some, some, sum_send.at[turn, 0]).wait()
        some = line.at[turn, pl.ds(0, wide - 1)]
        pltpu.make_async_copy(some, some, sum_send.at[turn, 1]).wait()


def store_pieces(solution_field, direction, checksum_weights, holder):
    width = lax.axis_size("wide")
    position = lax.axis_index("wide")
    weights_float = checksum_weights.astype(jnp.float32)
    scales = 1.0 / jnp.sqrt(jnp.sum(weights_float * weights_float, axis=1))
    scaled_weights = weights_float * scales[:, None]
    checks_count = checksum_weights.shape[0]
    flat = jnp.stack([solution_field, direction]).reshape(2, -1)
    cells = flat.shape[1]
    mine = lax.dynamic_slice_in_dim(scaled_weights, position, 1, 1)[:, 0]
    terms = (flat[:, None, :] * mine[None, :, None]).reshape(2 * checks_count, cells)
    piece = lax.psum_scatter(terms, "wide", scatter_dimension=1, tiled=True)
    index_range = jnp.arange(width, dtype=jnp.int32)
    same = holder[:, None] == holder[None, :]
    earlier = index_range[:, None] < index_range[None, :]
    slots = jnp.sum((same & earlier).astype(jnp.int32), axis=0)
    slot_range = jnp.arange(HOLD, dtype=jnp.int32)
    select = ((holder[None, :] == position) & (slots[None, :] == slot_range[:, None])).astype(
        jnp.float32
    )
    target = (index_range == holder[position]).astype(jnp.float32)
    outgoing = target[:, None, None] * piece[None, :, :]
    arrived = lax.all_to_all(outgoing, "wide", split_axis=0, concat_axis=0, tiled=True)
    return jnp.einsum("sj,jfc->sfc", select, arrived, precision=lax.Precision.HIGHEST)


def body(right_side, conductivity, checksum_weights, holder):
    wide, deep = lax.axis_size("wide"), lax.axis_size("deep")
    planes, rows, cols = conductivity.shape
    cells = planes * rows * cols
    pieces = cells == wide * wide * LANES and checksum_weights.shape[0] == 2 and HOLD == 2
    block = jax.ShapeDtypeStruct(conductivity.shape, jnp.float32)
    vmem = pl.BlockSpec(memory_space=pltpu.VMEM)
    smem = pl.BlockSpec(memory_space=pltpu.SMEM)
    tall = (planes + 2, rows + 2 * PAD, cols)
    scratch = [
        pltpu.VMEM((4,) + tall, jnp.float32),
        pltpu.VMEM(tall, jnp.float32),
        pltpu.VMEM(tall, jnp.float32),
        pltpu.SemaphoreType.DMA((4, 8)),
        pltpu.SemaphoreType.DMA((4, 8)),
        pltpu.VMEM((ITERS, deep, 1, LANES), jnp.float32),
        pltpu.VMEM((ITERS, wide, 1, LANES), jnp.float32),
        pltpu.SemaphoreType.DMA((ITERS, 2)),
        pltpu.SemaphoreType.DMA((ITERS, 2)),
    ]
    last = block
    if pieces:
        last = jax.ShapeDtypeStruct((8, wide * LANES), jnp.float32)
        scratch += [
            pltpu.VMEM((2, cols // LANES, planes * rows, LANES), jnp.float32),
            pltpu.VMEM((wide, 2 * wide, LANES), jnp.float32),
            pltpu.VMEM((wide, 2 * wide, LANES), jnp.float32),
            pltpu.VMEM((4 * wide, LANES), jnp.float32),
            pltpu.VMEM((8 * wide, LANES), jnp.float32),
            pltpu.VMEM((8 * wide, 4 * wide), jnp.float32),
            pltpu.VMEM((8, wide * LANES), jnp.float32),
            pltpu.SemaphoreType.DMA((2,)),
            pltpu.SemaphoreType.DMA((2,)),
        ]
    solution_field, residual, rest = pl.pallas_call(
        functools.partial(kernel, wide, deep, pieces),
        out_shape=[block, block, last],
        in_specs=[vmem, vmem, smem, smem],
        out_specs=[vmem, vmem, vmem],
        scratch_shapes=scratch,
        compiler_params=pltpu.CompilerParams(
            collective_id=0, has_side_effects=True, vmem_limit_bytes=32 * 1024 * 1024
        ),
    )(right_side, conductivity, checksum_weights, holder)
    if pieces:
        stored = rest.reshape(HOLD, 4, wide * LANES)
    else:
        stored = store_pieces(solution_field, rest, checksum_weights, holder)
    return (solution_field, residual, stored)


def solution(mesh):
    placed = (P("wide", "deep", None), P("wide", "deep", None), P(), P())
    return jax.shard_map(
        body,
        mesh=mesh,
        in_specs=placed,
        out_specs=(P("wide", "deep", None), P("wide", "deep", None), P("wide", None, "deep")),
        check_vma=False,
    )
```

time: 742 us -> 53.8 us (0.07)
  waiting for transfers between devices: 376 us -> 0 us
  blocking collectives: 253 us -> 0 us
  Pallas kernels: 0 us -> 47.8 us
  starting transfers between devices: 46.8 us -> 0 us
  other arithmetic: 23.8 us -> 0 us
  between operations: 22.6 us -> 0.65 us
  local copies, waits for them, and re-layouts: 17.6 us -> 5.09 us
    unnamed x2 -> x0, waiting for transfers between devices: 346 us -> none
    psum x6 -> x0, blocking collectives: 253 us -> none  [the longest x4 163 us: classic_norm(): return lax.psum(jnp.sum(residual * precond), ('wide', 'deep'))]
    pallas_call x0 -> x1, Pallas kernels: none -> 47.8 us  [body(): pl.pallas_call(functools.partial(kernel, wide, deep, pieces), out_shape=[...]
    ppermute x16 -> x0, starting transfers between devices: 35.5 us -> none  [the longest x8 25.2 us: with_halo(): before = lax.ppermute(last, axis, up)]
    ppermute x16 -> x0, waiting for transfers between devices: 15.2 us -> none  [the longest x8 9.02 us: with_halo(): after = lax.ppermute(leading, axis, down)]
    reduce_sum x8 -> x0, other arithmetic: 14.9 us -> none  [the longest x3 7.83 us: body(): jnp.sum(direction * image)]
    all_to_all x1 -> x0, waiting for transfers between devices: 14.7 us -> none  [body(): lax.all_to_all(outgoing, 'wide', split_axis=0, concat_axis=0, tiled=True)]
    all_to_all x1 -> x0, starting transfers between devices: 11.2 us -> none  [body(): lax.all_to_all(outgoing, 'wide', split_axis=0, concat_axis=0, tiled=True)]
  transfers between devices with their start and end apart: 18 -> 0, of which waited for: 12 -> 0; matrix products, arithmetic and copies ran while one was open for 1% -> 0% of each run, Pallas kernels for 0% -> 0%
where the time goes in v1:
time: 53.8 us; the launch traced here: 53.6 us
  Pallas kernels  47.8 us (89%)
  local copies, waits for them, and re-layouts  5.09 us (9%)
  between operations  0.65 us (1%)
    pallas_call x1, Pallas kernels, body(): pl.pallas_call(functools.partial(kernel, wide, deep, pieces), out_shape=[...  47.8 us
    unnamed x10, local copies, waits for them, and re-layouts  4.44 us

profile of v1, /device:TPU:0, one launch (start us, length us, event | category | flops | bytes accessed | tf_op | source)
XLA Modules:
  0.0 53.6 jit_solution(5855007924805723251)
XLA Ops:
  0.6 0.0 copy-start
  0.6 0.9 %copy-done = f32[2,64,256]{2,1,0:T(8,128)S(1)} copy-done((f32[2,64,256]{2,1,0:T(8,128)S(1)}, f32[2,64,256]{2,1,0:T(8,128)}, u32[]{:S(2)}) %copy-start) | copy-done | bytes 131096
  1.5 0.0 copy-start.1
  1.5 0.9 %copy-done.1 = f32[2,64,256]{2,1,0:T(8,128)S(1)} copy-done((f32[2,64,256]{2,1,0:T(8,128)S(1)}, f32[2,64,256]{2,1,0:T(8,128)}, u32[]{:S(2)}) %copy-start.1) | copy-done | bytes 131096
  2.4 0.0 copy-start.2
  2.4 0.7 %copy-done.2 = s32[2,16]{1,0:T(2,128)S(1)} copy-done((s32[2,16]{1,0:T(2,128)S(1)}, s32[2,16]{1,0:T(2,128)}, u32[]{:S(2)}) %copy-start.2) | copy-done | bytes 152
  3.1 0.0 copy-start.3
  3.1 0.7 %copy-done.3 = s32[16]{0:T(128)S(1)} copy-done((s32[16]{0:T(128)S(1)}, s32[16]{0:T(128)}, u32[]{:S(2)}) %copy-start.3) | copy-done | bytes 88
  3.8 47.8 %shard_map.67 = (f32[2,64,256]{2,1,0:T(8,128)S(1)}, f32[2,64,256]{2,1,0:T(8,128)S(1)}, f32[8,2048]{1,0:T(8,128)S(1)}) custom-call(f32[2,64,256]{2,1,0:T(8,128)S(1)} %copy-done, f32[2,64,256]{2,1,0:T(8,128)S(1)} %copy-done.1, s32[2,16]{1,0:T(2,128)S(1)} %copy-done.2, s32[16]{0:T(128)S(1)} %copy-done.3), custom_call_target="tpu_custom_call" | custom-call | tf_op jit(solution)/shard_map/pallas_call | solution.py:376
  51.6 0.7 %reshape.9 = f32[2,4,2048]{2,1,0:T(4,128)} reshape(f32[8,2048]{1,0:T(8,128)S(1)} %get-tuple-element.8) | data formatting | bytes 131072 | tf_op jit(solution)/shard_map/reshape | solution.py:387
  52.3 0.7 %copy.9 = f32[2,64,256]{2,1,0:T(8,128)} copy(f32[2,64,256]{2,1,0:T(8,128)S(1)} %get-tuple-element.12) | data formatting | bytes 262144
  52.9 0.7 %copy.10 = f32[2,64,256]{2,1,0:T(8,128)} copy(f32[2,64,256]{2,1,0:T(8,128)S(1)} %get-tuple-element.13) | data formatting | bytes 262144
Async XLA Ops:
  0.6 0.9 %copy-start = (f32[2,64,256]{2,1,0:T(8,128)S(1)}, f32[2,64,256]{2,1,0:T(8,128)}, u32[]{:S(2)}) copy-start(f32[2,64,256]{2,1,0:T(8,128)} %refs_0_.1) | copy-start | bytes 393220
  1.5 0.9 %copy-start.1 = (f32[2,64,256]{2,1,0:T(8,128)S(1)}, f32[2,64,256]{2,1,0:T(8,128)}, u32[]{:S(2)}) copy-start(f32[2,64,256]{2,1,0:T(8,128)} %refs_1_.1) | copy-start | bytes 393220
  2.4 0.7 %copy-start.2 = (s32[2,16]{1,0:T(2,128)S(1)}, s32[2,16]{1,0:T(2,128)}, u32[]{:S(2)}) copy-start(s32[2,16]{1,0:T(2,128)} %refs_2_.1) | copy-start | bytes 388
  3.1 0.7 %copy-start.3 = (s32[16]{0:T(128)S(1)}, s32[16]{0:T(128)}, u32[]{:S(2)}) copy-start(s32[16]{0:T(128)} %refs_3_.1) | copy-start | bytes 196

commit v2 on v1

--- a/solution.py
+++ b/solution.py
@@ -32,10 +32,20 @@
 
 
 def kernel(wide, deep, pieces, *refs):
-    r_ref, k_ref, w_ref, h_ref = refs[:4]
+    r_in, k_in, w_in, h_in = refs[:4]
     x_out, res_out, last_out = refs[4:7]
     (ext, zed, dirn, halo_send, halo_recv, pair, line, sum_send, sum_recv) = refs[7:16]
-    planes, rows, cols = k_ref.shape
+    r_ref, w_ref, h_ref, load_sem = refs[16:20]
+    planes, rows, cols = r_ref.shape
+    inner = (pl.ds(1, planes), pl.ds(PAD, rows))
+    loads = [
+        pltpu.make_async_copy(k_in, ext.at[(0,) + inner], load_sem.at[0]),
+        pltpu.make_async_copy(r_in, r_ref, load_sem.at[1]),
+        pltpu.make_async_copy(w_in, w_ref, load_sem.at[2]),
+        pltpu.make_async_copy(h_in, h_ref, load_sem.at[3]),
+    ]
+    for load in loads:
+        load.start()
     w = lax.axis_index("wide")
     d = lax.axis_index("deep")
 
@@ -63,7 +73,53 @@
         def _():
             pl.semaphore_signal(barrier, inc=1, device_id=(w + dx, d + dy), device_id_type=MESH)
 
-    for phase in range(4):
+    def halo_copy(phase, side):
+        dx, dy = SIDES[side]
+        return pltpu.make_async_remote_copy(
+            src_ref=ext.at[phase, span(dx, True, planes), rows_of(dy, True, rows)],
+            dst_ref=ext.at[phase, span(dx, False, planes), rows_of(dy, False, rows)],
+            send_sem=halo_send.at[phase, side],
+            recv_sem=halo_recv.at[phase, side],
+            device_id=(w + dx, d + dy),
+            device_id_type=MESH,
+        )
+
+    def halo_start(phase):
+        for side, (dx, dy) in enumerate(SIDES):
+
+            @pl.when(there(dx, dy))
+            def _():
+                halo_copy(phase, side).start()
+
+    def halo_wait(phase):
+        for side, (dx, dy) in enumerate(SIDES):
+
+            @pl.when(there(-dx, -dy))
+            def _():
+                halo_copy(phase, side).wait_recv()
+
+    def halo_sent(phase):
+        for side, (dx, dy) in enumerate(SIDES):
+
+            @pl.when(there(dx, dy))
+            def _():
+                halo_copy(phase, side).wait_send()
+
+    col = lax.broadcasted_iota(jnp.int32, (rows, cols), 1)
+
+    def smooth(block):
+        result = []
+        for x in range(planes):
+            t = 0.5 * (block[x] + block[x + 2]) + block[x + 1]
+            tall = t.shape[0]
+            t = 0.5 * (pltpu.roll(t, 1, 0) + pltpu.roll(t, tall - 1, 0)) + t
+            t = t[PAD:PAD + rows]
+            left = jnp.where(col == 0, 0.0, pltpu.roll(t, 1, 1))
+            right = jnp.where(col == cols - 1, 0.0, pltpu.roll(t, cols - 1, 1))
+            result.append(0.5 * (left + right) + t)
+        return result
+
+    def clear(phase):
         for dx, dy in SIDES:
 
             @pl.when(jnp.logical_not(there(-dx, -dy)))
@@ -71,11 +127,15 @@
                 at = (phase, span(dx, False, planes), rows_of(dy, False, rows))
                 ext[at] = jnp.zeros_like(ext[at])
 
-    inner = (slice(1, planes + 1), slice(PAD, PAD + rows))
-    ext[(0,) + inner] = k_ref[...]
-
+    loads[0].wait()
+    pl.semaphore_wait(barrier, greeted)
+    halo_start(0)
+    for phase in range(4):
+        clear(phase)
+    for load in loads[1:]:
+        load.wait()
     if pieces:
-        (field, parts, landed, sums, chosen, choose, final, all_send, all_recv) = refs[16:]
+        (field, parts, landed, sums, weigh, chosen, choose, final, all_send, all_recv) = refs[20:]
         lane = lax.broadcasted_iota(jnp.int32, (1, 4 * wide), 1)
         place = jnp.zeros((1, 4 * wide), jnp.int32)
         hold = [h_ref[j] for j in range(wide)]
@@ -88,60 +148,20 @@
         lane_no = lax.broadcasted_iota(jnp.int32, (8 * wide, 4 * wide), 1)
         hit = (line_no // 4 == place) & (line_no % 4 == lane_no // wide)
         choose[...] = jnp.where(hit, 1.0, 0.0).astype(jnp.float32)
-
-    def halo_copy(phase, side):
-        dx, dy = SIDES[side]
-        return pltpu.make_async_remote_copy(
-            src_ref=ext.at[phase, span(dx, True, planes), rows_of(dy, True, rows)],
-            dst_ref=ext.at[phase, span(dx, False, planes), rows_of(dy, False, rows)],
-            send_sem=halo_send.at[phase, side],
-            recv_sem=halo_recv.at[phase, side],
-            device_id=(w + dx, d + dy),
-            device_id_type=MESH,
-        )
-
-    def halo_start(phase):
-        for side, (dx, dy) in enumerate(SIDES):
-
-            @pl.when(there(dx, dy))
-            def _():
-                halo_copy(phase, side).start()
-
-    def halo_wait(phase):
-        for side, (dx, dy) in enumerate(SIDES):
-
-            @pl.when(there(-dx, -dy))
-            def _():
-                halo_copy(phase, side).wait_recv()
-
-    def halo_sent(phase):
-        for side, (dx, dy) in enumerate(SIDES):
-
-            @pl.when(there(dx, dy))
-            def _():
-                halo_copy(phase, side).wait_send()
-
-    col = lax.broadcasted_iota(jnp.int32, (rows, cols), 1)
-
-    def smooth(block):
-        result = []
-        for x in range(planes):
-            t = 0.5 * (block[x] + block[x + 2]) + block[x + 1]
-            tall = t.shape[0]
-            t = 0.5 * (pltpu.roll(t, 1, 0) + pltpu.roll(t, tall - 1, 0)) + t
-            t = t[PAD:PAD + rows]
-            left = jnp.where(col == 0, 0.0, pltpu.roll(t, 1, 1))
-            right = jnp.where(col == cols - 1, 0.0, pltpu.roll(t, cols - 1, 1))
-            result.append(0.5 * (left + right) + t)
-        return result
-
-    pl.semaphore_wait(barrier, greeted)
-    halo_start(0)
+        for k in range(2):
+            squares = jnp.int32(0)
+            for p in range(wide):
+                squares = squares + w_ref[k, p] * w_ref[k, p]
+            scale = 1.0 / jnp.sqrt(jnp.full((1, LANES), squares, jnp.int32).astype(jnp.float32))
+            for p in range(wide):
+                whole = jnp.full((1, LANES), w_ref[k, p], jnp.int32).astype(jnp.float32)
+                weigh[k, p:p + 1] = whole * scale
+
     halo_wait(0)
 
     kappa = [ext[0, x] for x in range(planes + 2)]
     blurred = smooth(kappa)
-    mine = [k_ref[x] for x in range(planes)]
+    mine = [kappa[x + 1][PAD:PAD + rows] for x in range(planes)]
     diagonal = [6.0 * mine[x] + blurred[x] for x in range(planes)]
     inverse = [1.0 / diagonal[x] for x in range(planes)]
     for x in range(planes):
@@ -199,7 +219,7 @@
         second = smooth([ext[0, x] * block[x] for x in range(planes + 2)])
         image, spread = [], []
         for x in range(planes):
-            k = k_ref[x]
+            k = ext[0, x + 1, PAD:PAD + rows]
             image.append((diagonal[x] + 2.0 * k) * own[x] - k * first[x] - second[x])
             spread.append(image[x] * inverse[x])
         carries_on = turn < ITERS - 1
@@ -250,29 +270,24 @@
                     f, c % halves, pl.ds(c // halves, wide, stride=stride), :]
         landed[w] = parts[w]
 
-        def scatter(i, carry):
-            q = lax.rem(w + i, wide)
-            pltpu.make_async_remote_copy(
+        def scatter(q):
+            return pltpu.make_async_remote_copy(
                 src_ref=parts.at[q], dst_ref=landed.at[w],
                 send_sem=all_send.at[0], recv_sem=all_recv.at[0],
                 device_id=(q, d), device_id_type=MESH,
-            ).start()
-            return carry
-
-        lax.fori_loop(1, wide, scatter, 0)
+            )
+
+        for i in range(1, wide):
+            scatter(jnp.bitwise_xor(w, i)).start()
         some = landed.at[pl.ds(0, wide - 1)]
         pltpu.make_async_copy(some, some, all_recv.at[0]).wait()
         for k in range(2):
-            squares = jnp.int32(0)
-            for p in range(wide):
-                squares = squares + w_ref[k, p] * w_ref[k, p]
-            scale = 1.0 / jnp.sqrt(jnp.full((1, LANES), squares.astype(jnp.float32)))
             for f in range(2):
                 total = jnp.zeros((wide, LANES), jnp.float32)
                 for p in range(wide):
-                    total = total + w_ref[k, p].astype(jnp.float32) * landed[p, f * wide:(f + 1) * wide]
+                    total = total + weigh[k, p:p + 1] * landed[p, f * wide:(f + 1) * wide]
                 at = (2 * f + k) * wide
-                sums[at:at + wide] = total * scale
+                sums[at:at + wide] = total
         chosen[...] = jnp.dot(
             choose[...], sums[...], precision=lax.Precision.HIGHEST,
             preferred_element_type=jnp.float32)
@@ -295,7 +310,8 @@
         lax.fori_loop(1, wide, deliver, 0)
         some = final.at[:, pl.ds(0, (wide - 1) * LANES)]
         pltpu.make_async_copy(some, some, all_recv.at[1]).wait()
-        last_out[...] = final[...]
+        last_out[0] = final[0:4]
+        last_out[1] = final[4:8]
         some = parts.at[pl.ds(0, wide - 1)]
         pltpu.make_async_copy(some, some, all_send.at[0]).wait()
         some = chosen.at[pl.ds(0, (wide - 1) * 8)]
@@ -343,10 +359,10 @@
     wide, deep = lax.axis_size("wide"), lax.axis_size("deep")
     planes, rows, cols = conductivity.shape
     cells = planes * rows * cols
-    pieces = cells == wide * wide * LANES and checksum_weights.shape[0] == 2 and HOLD == 2
+    pieces = cells == wide * wide * LANES and wide & (wide - 1) == 0 and checksum_weights.shape[0] == 2 and HOLD == 2
     block = jax.ShapeDtypeStruct(conductivity.shape, jnp.float32)
     vmem = pl.BlockSpec(memory_space=pltpu.VMEM)
-    smem = pl.BlockSpec(memory_space=pltpu.SMEM)
+    anywhere = pl.BlockSpec(memory_space=pltpu.HBM)
     tall = (planes + 2, rows + 2 * PAD, cols)
     scratch = [
         pltpu.VMEM((4,) + tall, jnp.float32),
@@ -358,33 +374,42 @@
         pltpu.VMEM((ITERS, wide, 1, LANES), jnp.float32),
         pltpu.SemaphoreType.DMA((ITERS, 2)),
         pltpu.SemaphoreType.DMA((ITERS, 2)),
+        pltpu.VMEM(conductivity.shape, jnp.float32),
+        pltpu.SMEM(checksum_weights.shape, jnp.int32),
+        pltpu.SMEM(holder.shape, jnp.int32),
+        pltpu.SemaphoreType.DMA((4,)),
     ]
     last = block
     if pieces:
-        last = jax.ShapeDtypeStruct((8, wide * LANES), jnp.float32)
+        last = jax.ShapeDtypeStruct((HOLD, 4, wide * LANES), jnp.float32)
         scratch += [
             pltpu.VMEM((2, cols // LANES, planes * rows, LANES), jnp.float32),
             pltpu.VMEM((wide, 2 * wide, LANES), jnp.float32),
             pltpu.VMEM((wide, 2 * wide, LANES), jnp.float32),
             pltpu.VMEM((4 * wide, LANES), jnp.float32),
+            pltpu.VMEM((2, wide, LANES), jnp.float32),
             pltpu.VMEM((8 * wide, LANES), jnp.float32),
             pltpu.VMEM((8 * wide, 4 * wide), jnp.float32),
             pltpu.VMEM((8, wide * LANES), jnp.float32),
             pltpu.SemaphoreType.DMA((2,)),
             pltpu.SemaphoreType.DMA((2,)),
         ]
+    arguments = [
+        pltpu.with_memory_space_constraint(a, pltpu.HBM)
+        for a in (right_side, conductivity, checksum_weights, holder)
+    ]
     solution_field, residual, rest = pl.pallas_call(
         functools.partial(kernel, wide, deep, pieces),
         out_shape=[block, block, last],
-        in_specs=[vmem, vmem, smem, smem],
+        in_specs=[anywhere] * 4,
         out_specs=[vmem, vmem, vmem],
         scratch_shapes=scratch,
         compiler_params=pltpu.CompilerParams(
-            collective_id=0, has_side_effects=True, vmem_limit_bytes=32 * 1024 * 1024
+            collective_id=0, has_side_effects=True, vmem_limit_bytes=24 * 1024 * 1024
         ),
-    )(right_side, conductivity, checksum_weights, holder)
+    )(*arguments)
     if pieces:
-        stored = rest.reshape(HOLD, 4, wide * LANES)
+        stored = rest
     else:
         stored = store_pieces(solution_field, rest, checksum_weights, holder)
     return (solution_field, residual, stored)

time: 53.8 us -> 49.2 us (0.914)
  local copies, waits for them, and re-layouts: 5.09 us -> 1.94 us
  Pallas kernels: 47.8 us -> 46.5 us
    unnamed x10 -> x3, local copies, waits for them, and re-layouts: 4.44 us -> 1.94 us
    pallas_call x1, Pallas kernels: 47.8 us -> 46.5 us  [body(): pl.pallas_call(functools.partial(kernel, wide, deep, pieces), out_shape=[...]
    reshape x1 -> x0, local copies, waits for them, and re-layouts: 0.65 us -> none  [body(): stored = rest.reshape(HOLD, 4, wide * LANES)]
where the time goes in v2:
time: 49.2 us; the launch traced here: 49.1 us
  Pallas kernels  46.5 us (95%)
  local copies, waits for them, and re-layouts  1.94 us (4%)
  between operations  0.64 us (1%)
    pallas_call x1, Pallas kernels, body(): pl.pallas_call(functools.partial(kernel, wide, deep, pieces), out_shape=[...  46.5 us
    unnamed x3, local copies, waits for them, and re-layouts  1.94 us

profile of v2, /device:TPU:0, one launch (start us, length us, event | category | flops | bytes accessed | tf_op | source)
XLA Modules:
  0.0 49.1 jit_solution(11148004265647428225)
XLA Ops:
  0.6 46.5 %shard_map.67 = (f32[2,64,256]{2,1,0:T(8,128)S(1)}, f32[2,64,256]{2,1,0:T(8,128)S(1)}, f32[2,4,2048]{2,1,0:T(4,128)S(1)}) custom-call(f32[2,64,256]{2,1,0:T(8,128)} %refs_0_.1, f32[2,64,256]{2,1,0:T(8,128)} %refs_1_.1, s32[2,16]{1,0:T(2,128)} %refs_2_.1, s32[16]{0:T(128)} %refs_3_.1), custom_call_target="tpu_custom_call" | custom-call | tf_op jit(solution)/shard_map/pallas_call | solution.py:401
  47.2 0.7 %copy.10 = f32[2,64,256]{2,1,0:T(8,128)} copy(f32[2,64,256]{2,1,0:T(8,128)S(1)} %get-tuple-element.6) | data formatting | bytes 262144
  47.8 0.7 %copy.11 = f32[2,64,256]{2,1,0:T(8,128)} copy(f32[2,64,256]{2,1,0:T(8,128)S(1)} %get-tuple-element.7) | data formatting | bytes 262144
  48.5 0.6 %copy.12 = f32[2,4,2048]{2,1,0:T(4,128)} copy(f32[2,4,2048]{2,1,0:T(4,128)S(1)} %get-tuple-element.8) | data formatting | bytes 131072
